TPU v7x, 32 devices: a whole 2x2x4 slice. The times are simulated.
32 devices in a mesh: doc: 8 (over y, x, core), term: 4 (over z).
Axes of the slice: x: 2, y: 2, z: 4, core: 2. Of those that a mesh axis runs over, the one named last changes fastest.
Arguments:
- doc_tiles: bfloat16 [1024, 24, 2048], P('doc', None, 'term'), may hold values from -8 to 8
- tile_list: int32 [8, 24], replicated, may hold values from 0 to 127, as said below
Outputs:
- cosine: float32 [1024, 1024], P(('doc', 'term'))
Inputs may be any that keep to these rules, and one draw needn't show every extreme that they name: `tile_list`: each row names 24 different term blocks.
All inputs are finite; a program needn't handle non-finite values.
Results may differ from a plain program's by a relative error of at most 0.0003.
Values may be sent and summed in bfloat16 or wider, within the bound.
A program may use at most 64 MiB of HBM per device.

v0:
```python
import functools

import jax
import jax.numpy as jnp
from jax import lax
from jax.experimental import pallas as pl
from jax.experimental.pallas import tpu as pltpu
from jax.sharding import PartitionSpec as P

epsilon = 1e-06
LANES = 128
MESH = pl.DeviceIdType.MESH


def flip(g, o):
    bit = 1
    while bit <= o:
        if o & bit:
            g = g + bit - 2 * bit * lax.rem(lax.div(g, bit), 2)
        bit *= 2
    return g


class Plan:
    def __init__(self, D, T, R, N, W):
        G = 1
        while D % (2 * G) == 0 and W % (2 * G * LANES) == 0:
            G *= 2
        self.D, self.T, self.R, self.N, self.W, self.G = D, T, R, N, W, G
        self.M = D // G
        self.L = W // G
        self.SR = R // T
        self.mirrored = (
            G > 1 and self.M % 2 == 0 and R == LANES and self.SR % T == 0 and self.SR // T % 8 == 0
        )
        self.H = self.M // 2 if self.mirrored else self.M
        self.parts = 2 if N % 2 == 0 else 1
        self.step = N // self.parts
        self.rows = 16 if R % 16 == 0 else R

    def count(self, o):
        return self.M if o == 0 else self.H

    def stage(self, o):
        return 0 if o == 0 else 1 if o & (o - 1) == 0 else 2


def body(plan, names, docs, out, *scratch):
    D, T, G, M, H = plan.D, plan.T, plan.G, plan.M, plan.H
    R, N, L, SR = plan.R, plan.N, plan.L, plan.SR
    scratch = list(scratch)
    take = lambda n: [scratch.pop(0) for _ in range(n)]
    tiles = take(G)
    part = {(a, b): take(1)[0] for a in range(G) for b in range(G)}
    got = {(a, b): take(1)[0] for a in range(1, G) for b in range(G)}
    whole = {b: take(1)[0] for b in range(G)}
    got_z = {b: take(1)[0] for b in range(G)}
    if plan.mirrored:
        turned = {b: take(1)[0] for b in range(1, G)}
        mirror = {b: take(1)[0] for b in range(1, G)}
    raw = take(G)
    ranges = [None] + take(G - 1)
    order, sq_term, sq_doc, table_rows, table = take(5)
    (
        raw_sem, table_sem, send_a, recv_a, send_f, send_st, recv_st, send_sd, recv_sd,
        send_p, recv_p, send_m, recv_m, send_z, recv_z,
    ) = scratch

    d = lax.axis_index("doc")
    t = lax.axis_index("term")
    g = lax.div(d, M)
    m = lax.rem(d, M)
    groups = [flip(g, o) for o in range(G)]

    def doc_peer(o):
        return lax.rem(d + o, D)

    def term_peer(o):
        return lax.rem(t + o, T)

    def sibling(i):
        return lax.rem(m + i, M)

    def remote(src, dst, ssem, rsem, doc, term):
        return pltpu.make_async_remote_copy(
            src_ref=src, dst_ref=dst, send_sem=ssem, recv_sem=rsem,
            device_id=(doc, term), device_id_type=MESH,
        )

    def column_member(row_group, column_group, i):
        if not plan.mirrored:
            return i
        return 2 * i + lax.rem(m + jnp.where(row_group < column_group, 1, 0), 2)

    parts, step = plan.parts, plan.step

    def slot(o, member, h):
        return tiles[o].at[pl.ds(member * (N + 1) + h * step, step)]

    def cut(group):
        if G == 1:
            return docs
        return docs.at[:, pl.ds(pl.multiple_of(group * L, L), L)]

    first = [o for o in range(1, G) if plan.stage(o) == 1]
    second = [o for o in range(1, G) if plan.stage(o) == 2]
    loads = {}
    for o in first + [0] + second:
        loads[o] = pltpu.make_async_copy(cut(groups[o]), raw[o], raw_sem.at[o])
        loads[o].start()

    barrier = pltpu.get_barrier_semaphore()
    greeted = [
        (o, u) for o in range(D) for u in range(T) if o + u and (plan.mirrored or not o * u)
    ]
    for o, u in greeted:
        pl.semaphore_signal(
            barrier, inc=1, device_id=(doc_peer(o), term_peer(u)), device_id_type=MESH
        )
    if greeted:
        pl.semaphore_wait(barrier, len(greeted))

    pending = []

    def begin(copy):
        copy.start()
        pending.append(copy)
        return copy

    def send_range(o, h):
        return begin(
            remote(
                ranges[o].at[pl.ds(h * step, step)], slot(o, m, h), send_a.at[o, h],
                recv_a.at[o, m, h], groups[o] * M + m, t,
            )
        )

    def hand_on(o, h):
        for i in range(1, M):
            begin(
                remote(
                    slot(o, m, h), slot(o, m, h), send_f.at[o, i, h], recv_a.at[o, m, h],
                    g * M + sibling(i), t,
                )
            )

    def take_over(o):
        for h in range(parts):
            for i in range(1, M):
                other = sibling(i)
                remote(
                    slot(o, other, h), slot(o, other, h), send_f.at[o, i, h], recv_a.at[o, other, h],
                    g * M + other, t,
                ).wait_recv()

    def arrived(o, h):
        remote(
            slot(o, m, h), slot(o, m, h), send_a.at[o, h], recv_a.at[o, m, h], groups[o] * M + m, t
        ).wait_recv()
        hand_on(o, h)

    def slots_first(o):
        loads[o].wait()

        def some_rows(k, carry):
            rows = pl.ds(pl.multiple_of(k * plan.rows, plan.rows), plan.rows)
            held = raw[o][pl.ds(pl.multiple_of(k * plan.rows * N, plan.rows * N), plan.rows * N), :]
            value = jnp.dot(order[...], held, preferred_element_type=jnp.float32)
            value = value.astype(docs.dtype).reshape(N, plan.rows, L)
            if o:
                ranges[o][:, rows, :] = value
            else:
                tiles[0][pl.ds(m * (N + 1), N), rows, :] = value
            return carry

        lax.fori_loop(0, R // plan.rows, some_rows, 0)

    size = plan.rows * N
    spot = lax.broadcasted_iota(jnp.int32, (size, size), 0)
    origin = lax.rem(spot, plan.rows) * N + lax.div(spot, plan.rows)
    hit = origin == lax.broadcasted_iota(jnp.int32, (size, size), 1)
    order[...] = jnp.where(hit, 1.0, 0.0).astype(docs.dtype)

    first_sends = []
    for o in first:
        slots_first(o)
        for h in range(parts):
            first_sends.append(send_range(o, h))
    slots_first(0)
    for h in range(parts):
        hand_on(0, h)
    for o in second:
        slots_first(o)
        for h in range(parts - 1):
            send_range(o, h)

    for o in range(G):
        tiles[o][m * (N + 1) + N] = jnp.zeros((R, L), docs.dtype)
    same = lax.broadcasted_iota(jnp.int32, (N, N), 0) == lax.broadcasted_iota(jnp.int32, (N, N), 1)
    place = lax.broadcasted_iota(jnp.int32, (N, N), 0)
    for a in range(G):
        line = names[pl.ds(groups[a] * M + m, 1), :]
        upright = jnp.sum(jnp.where(same, line, 0), axis=1, keepdims=True)
        for c in range(D):
            found = jnp.where(upright == names[c : c + 1, :], place, N)
            table_rows[a * D + c : a * D + c + 1, 0:N] = jnp.min(found, axis=0, keepdims=True)
    to_scalars = pltpu.make_async_copy(table_rows, table, table_sem)
    to_scalars.start()

    def add_square(a, total):
        for q in range(G):
            held = ranges[q][a] if q else tiles[0][m * (N + 1) + a]
            value = held.astype(jnp.float32)
            total = total + value * value
        return total

    square = lax.fori_loop(0, N, add_square, jnp.zeros((R, L), jnp.float32))
    column = jnp.sum(square, axis=1, keepdims=True)
    eye = lax.broadcasted_iota(jnp.int32, (R, R), 0) == lax.broadcasted_iota(jnp.int32, (R, R), 1)
    row = jnp.sum(jnp.where(eye, column, 0.0), axis=0, keepdims=True)
    sq_term[t] = jnp.broadcast_to(row, (8, R))
    for o in range(1, T):
        begin(remote(sq_term.at[t], sq_term.at[t], send_st.at[o], recv_st.at[t], d, term_peer(o)))
    for o in range(1, T):
        p = term_peer(o)
        remote(sq_term.at[p], sq_term.at[p], send_st.at[o], recv_st.at[p], d, p).wait_recv()
    total = sq_term[0]
    for q in range(1, T):
        total = total + sq_term[q]
    sq_doc[d] = total
    for o in range(1, D):
        begin(remote(sq_doc.at[d], sq_doc.at[d], send_sd.at[o], recv_sd.at[d], doc_peer(o), t))

    def pair(a, b):
        def one(i, carry):
            member = i if a == b else column_member(groups[a], groups[b], i)
            line = a * D + groups[b] * M + member
            left = jnp.concatenate(
                [tiles[a][m * (N + 1) + table[line, e]] for e in range(N)], axis=1
            )
            right = jnp.concatenate([tiles[b][member * (N + 1) + e] for e in range(N)], axis=1)
            part[a, b][i] = lax.dot_general(
                left, right, (((1,), (1,)), ((), ())), preferred_element_type=jnp.float32
            )
            return carry

        number = plan.count(a ^ b)
        if number == 1:
            one(0, 0)
        else:
            lax.fori_loop(0, number, one, 0)
        if a:
            begin(
                remote(
                    part[a, b], got[a, b], send_p.at[a, b], recv_p.at[a, b], groups[a] * M + m, t
                )
            )

    wanted = list(range(1, G)) + [0]

    def pairs(stage):
        todo = [
            (a, b)
            for a in range(G)
            for b in range(G)
            if max(plan.stage(a), plan.stage(b)) == stage
        ]
        for a, b in sorted(todo, key=lambda ab: (wanted.index(ab[0] ^ ab[1]), -ab[0])):
            pair(a, b)

    to_scalars.wait()
    take_over(0)
    pairs(0)
    for h in range(parts):
        for o in first:
            arrived(o, h)
    for copy in first_sends:
        copy.wait_send()
        pending.remove(copy)
    for o in second:
        send_range(o, parts - 1)
    for o in first:
        take_over(o)
    if first:
        pairs(1)
    for h in range(parts):
        for o in second:
            arrived(o, h)
    for o in second:
        take_over(o)
    if second:
        pairs(2)

    def over_term(source, landing, ssem, rsem):
        for o in range(1, T):
            p = term_peer(o)
            begin(
                remote(
                    source.at[:, pl.ds(p * SR, SR), :], landing.at[o - 1], ssem.at[o], rsem.at[o], d, p
                )
            )

    for b in wanted:
        for a in range(1, G):
            remote(
                part[a, a ^ b], got[a, a ^ b], send_p.at[a, a ^ b], recv_p.at[a, a ^ b],
                groups[a] * M + m, t,
            ).wait_recv()
        for i in range(plan.count(b)):
            total = part[0, b][i]
            for a in range(1, G):
                total = total + got[a, a ^ b][i]
            whole[b][i] = total
        over_term(whole[b], got_z[b], send_z.at[b], recv_z.at[b])

    def mirror_member(b, i):
        return 2 * i + lax.rem(m + jnp.where(groups[b] < g, 1, 0), 2)

    lane_set = lax.div(lax.broadcasted_iota(jnp.int32, (max(SR // T, 1), R), 1), SR)
    sums = {}
    for b in wanted:
        for o in range(1, T):
            remote(
                whole[b].at[:, pl.ds(t * SR, SR), :], got_z[b].at[o - 1], send_z.at[b, o],
                recv_z.at[b, o], d, term_peer(o),
            ).wait_recv()
        for i in range(plan.count(b)):
            total = whole[b][i, pl.ds(pl.multiple_of(t * SR, SR), SR), :]
            for o in range(1, T):
                total = total + got_z[b][o - 1, i]
            sums[b, i] = total
            if plan.mirrored and b:
                upright = jnp.concatenate([total] * T, axis=0).T
                size = SR // T
                for u in range(T):
                    packed = jnp.zeros((size, R), jnp.float32)
                    for k in range(T):
                        lines = upright[u * SR + k * size : u * SR + (k + 1) * size]
                        packed = jnp.where(lane_set == k, lines, packed)
                    turned[b][i, u] = packed
                for w in range(T):
                    u = term_peer(w)
                    begin(
                        remote(
                            turned[b].at[i, u], mirror[b].at[lax.div(m, 2), t], send_m.at[b, i, w],
                            recv_m.at[b, lax.div(m, 2), t],
                            groups[b] * M + column_member(g, groups[b], i), u,
                        )
                    )

    for o in range(1, D):
        p = doc_peer(o)
        remote(sq_doc.at[p], sq_doc.at[p], send_sd.at[o], recv_sd.at[p], p, t).wait_recv()
    pick = lax.broadcasted_iota(jnp.int32, (SR, R), 1) == (
        lax.broadcasted_iota(jnp.int32, (SR, R), 0) + t * SR
    )
    own_column = jnp.sum(jnp.where(pick, sq_doc[d][0:1], 0.0), axis=1, keepdims=True)
    row_norm = jnp.sqrt(own_column + epsilon)

    def finish(total, c):
        norms = row_norm * jnp.sqrt(sq_doc[c][0:1] + epsilon)
        out[:, pl.ds(pl.multiple_of(c * R, R), R)] = total / norms

    for b, i in sums:
        finish(sums[b, i], groups[b] * M + (column_member(g, groups[b], i) if b else i))
    if plan.mirrored:
        for b in range(1, G):
            for i in range(H):
                c = groups[b] * M + mirror_member(b, i)
                for u in range(T):
                    remote(
                        turned[b].at[i, u], mirror[b].at[i, u], send_m.at[b, i, u],
                        recv_m.at[b, i, u], c, t,
                    ).wait_recv()
                lines = []
                for k in range(T):
                    line = jnp.zeros((SR // T, R), jnp.float32)
                    for u in range(T):
                        piece = mirror[b][i, u]
                        if u != k:
                            piece = pltpu.roll(piece, (u - k) % T * SR, 1)
                        line = jnp.where(lane_set == u, piece, line)
                    lines.append(line)
                finish(jnp.concatenate(lines, axis=0), c)

    for copy in pending:
        copy.wait_send()


def shards(doc_tiles, tile_list):
    D = lax.axis_size("doc")
    T = lax.axis_size("term")
    R, N, W = doc_tiles.shape
    plan = Plan(D, T, R, N, W)
    G, M, H, L, SR = plan.G, plan.M, plan.H, plan.L, plan.SR
    many = lambda *shape: pltpu.SemaphoreType.DMA(shape)
    buffer = lambda *shape: pltpu.VMEM(tuple(max(n, 1) for n in shape), jnp.float32)
    scratch = [pltpu.VMEM((M * (N + 1), R, L), doc_tiles.dtype) for _ in range(G)]
    scratch += [buffer(plan.count(a ^ b), R, R) for a in range(G) for b in range(G)]
    scratch += [buffer(plan.count(a ^ b), R, R) for a in range(1, G) for b in range(G)]
    scratch += [buffer(plan.count(b), R, R) for b in range(G)]
    scratch += [buffer(T - 1, plan.count(b), SR, R) for b in range(G)]
    if plan.mirrored:
        scratch += [buffer(H, T, SR // T, R) for _ in range(1, G)]
        scratch += [buffer(H, T, SR // T, R) for _ in range(1, G)]
    scratch += [pltpu.VMEM((R * N, L), doc_tiles.dtype) for _ in range(G)]
    scratch += [pltpu.VMEM((N, R, L), doc_tiles.dtype) for _ in range(1, G)]
    scratch += [pltpu.VMEM((plan.rows * N, plan.rows * N), doc_tiles.dtype)]
    scratch += [buffer(T, 8, R), buffer(D, 8, R)]
    scratch += [pltpu.VMEM((G * D, LANES), jnp.int32), pltpu.SMEM((G * D, LANES), jnp.int32)]
    scratch += [
        many(G), pltpu.SemaphoreType.DMA,
        many(G, plan.parts), many(G, M, plan.parts), many(G, M, plan.parts),
        many(T), many(T), many(D), many(D),
        many(G, G), many(G, G), many(G, M, T), many(G, M, T),
        many(G, T), many(G, T),
    ]
    return pl.pallas_call(
        functools.partial(body, plan),
        out_shape=jax.ShapeDtypeStruct((SR, D * R), jnp.float32),
        in_specs=[
            pl.BlockSpec(memory_space=pltpu.VMEM),
            pl.BlockSpec(memory_space=pl.ANY),
        ],
        out_specs=pl.BlockSpec(memory_space=pltpu.VMEM),
        scratch_shapes=scratch,
        compiler_params=pltpu.CompilerParams(
            collective_id=0, has_side_effects=True, vmem_limit_bytes=56 * 1024 * 1024
        ),
        cost_estimate=pl.CostEstimate(
            flops=2 * G * R * D * R * N * L,
            bytes_accessed=R * N * W * 2 + SR * D * R * 4,
            transcendentals=0,
        ),
    )(tile_list, doc_tiles.reshape(R * N, W))


def solution(mesh):
    placed = (P("doc", None, "term"), P())
    return jax.shard_map(
        shards, mesh=mesh, in_specs=placed, out_specs=P(("doc", "term"), None), check_vma=False
    )
```

profile of v0, /device:TPU:0, one launch (start us, length us, event | category | flops | bytes accessed | tf_op | source)
XLA Modules:
  0.0 73.9 jit_solution(1811888814868497067)
XLA Ops:
  0.0 72.4 %shard_map.28 = f32[32,1024]{1,0:T(8,128)} custom-call(s32[8,24]{1,0:T(8,128)} %names.1, bf16[3072,512]{1,0:T(8,128)(2,1)} %bitcast.1), custom_call_target="tpu_custom_call" | custom-call | flops 3221225472 | bytes 3276800 | tf_op jit(solution)/shard_map/pallas_call | solution.py:418
  72.4 1.6 %copy.4 = f32[32,1024]{1,0:T(8,128)} copy(f32[32,1024]{1,0:T(8,128)} %shard_map.28) | data formatting | bytes 262144
where the time goes:
time: 74.1 us; the launch traced here: 73.9 us
  Pallas kernels  72.4 us (98%)
  local copies, waits for them, and re-layouts  1.57 us (2%)
    pallas_call x1, Pallas kernels, shards(): pl.pallas_call(functools.partial(body, plan), out_shape=jax.ShapeDtypeStr...  72.4 us
    unnamed x1, local copies, waits for them, and re-layouts  1.57 us

commit v1 on v0

--- a/solution.py
+++ b/solution.py
@@ -41,6 +41,28 @@
     def count(self, o):
         return self.M if o == 0 else self.H
 
+    def wave(self, a, b):
+        return max(self.stage(a), self.stage(b))
+
+    def term_first(self, a, b):
+        return a > 0 and (self.wave(a, b) == 1 or a == b)
+
+    def blocks(self, wave, a):
+        return [
+            (b, i)
+            for b in range(self.G)
+            if self.wave(a, b) == wave and self.term_first(a, b)
+            for i in range(self.count(a ^ b))
+        ]
+
+    def sets(self):
+        return [(w, a) for w in (1, 2) for a in range(1, self.G) if self.blocks(w, a)]
+
+    def direct(self):
+        return [
+            (a, b) for a in range(self.G) for b in range(self.G) if not self.term_first(a, b)
+        ]
+
     def stage(self, o):
         return 0 if o == 0 else 1 if o & (o - 1) == 0 else 2
 
@@ -51,8 +73,12 @@
     scratch = list(scratch)
     take = lambda n: [scratch.pop(0) for _ in range(n)]
     tiles = take(G)
-    part = {(a, b): take(1)[0] for a in range(G) for b in range(G)}
-    got = {(a, b): take(1)[0] for a in range(1, G) for b in range(G)}
+    part = {pair: take(1)[0] for pair in plan.direct()}
+    got = {pair: take(1)[0] for pair in plan.direct() if pair[0]}
+    early = {key: take(1)[0] for key in plan.sets()}
+    early_z = {key: take(1)[0] for key in plan.sets()}
+    early_sum = {key: take(1)[0] for key in plan.sets()}
+    early_xy = {key: take(1)[0] for key in plan.sets()}
     whole = {b: take(1)[0] for b in range(G)}
     got_z = {b: take(1)[0] for b in range(G)}
     if plan.mirrored:
@@ -63,7 +89,7 @@
     order, sq_term, sq_doc, table_rows, table = take(5)
     (
         raw_sem, table_sem, send_a, recv_a, send_f, send_st, recv_st, send_sd, recv_sd,
-        send_p, recv_p, send_m, recv_m, send_z, recv_z,
+        send_p, recv_p, send_m, recv_m, send_z, recv_z, send_ez, recv_ez, send_ex, recv_ex,
     ) = scratch
 
     d = lax.axis_index("doc")
@@ -117,9 +143,6 @@
         pl.semaphore_signal(
             barrier, inc=1, device_id=(doc_peer(o), term_peer(u)), device_id_type=MESH
         )
-    if greeted:
-        pl.semaphore_wait(barrier, len(greeted))
-
     pending = []
 
     def begin(copy):
@@ -176,14 +199,20 @@
         lax.fori_loop(0, R // plan.rows, some_rows, 0)
 
     size = plan.rows * N
-    spot = lax.broadcasted_iota(jnp.int32, (size, size), 0)
-    origin = lax.rem(spot, plan.rows) * N + lax.div(spot, plan.rows)
+    origin = jnp.concatenate(
+        [lax.broadcasted_iota(jnp.int32, (plan.rows, 1), 0) * N + a for a in range(N)], axis=0
+    )
     hit = origin == lax.broadcasted_iota(jnp.int32, (size, size), 1)
     order[...] = jnp.where(hit, 1.0, 0.0).astype(docs.dtype)
 
     first_sends = []
+    if first:
+        slots_first(first[0])
+    if greeted:
+        pl.semaphore_wait(barrier, len(greeted))
     for o in first:
-        slots_first(o)
+        if o != first[0]:
+            slots_first(o)
         for h in range(parts):
             first_sends.append(send_range(o, h))
     slots_first(0)
@@ -231,7 +260,22 @@
     for o in range(1, D):
         begin(remote(sq_doc.at[d], sq_doc.at[d], send_sd.at[o], recv_sd.at[d], doc_peer(o), t))
 
+    def over_term(source, landing, ssem, rsem):
+        for o in range(1, T):
+            p = term_peer(o)
+            begin(
+                remote(
+                    source.at[:, pl.ds(p * SR, SR), :], landing.at[o - 1], ssem.at[o], rsem.at[o], d, p
+                )
+            )
+
     def pair(a, b):
+        wave = plan.wave(a, b)
+        if plan.term_first(a, b):
+            target, base = early[wave, a], plan.blocks(wave, a).index((b, 0))
+        else:
+            target, base = part[a, b], 0
+
         def one(i, carry):
             member = i if a == b else column_member(groups[a], groups[b], i)
             line = a * D + groups[b] * M + member
@@ -239,7 +283,7 @@
                 [tiles[a][m * (N + 1) + table[line, e]] for e in range(N)], axis=1
             )
             right = jnp.concatenate([tiles[b][member * (N + 1) + e] for e in range(N)], axis=1)
-            part[a, b][i] = lax.dot_general(
+            target[base + i] = lax.dot_general(
                 left, right, (((1,), (1,)), ((), ())), preferred_element_type=jnp.float32
             )
             return carry
@@ -249,7 +293,12 @@
             one(0, 0)
         else:
             lax.fori_loop(0, number, one, 0)
-        if a:
+        if plan.term_first(a, b):
+            if plan.blocks(wave, a)[-1][0] == b:
+                over_term(
+                    early[wave, a], early_z[wave, a], send_ez.at[wave - 1, a], recv_ez.at[wave - 1, a]
+                )
+        elif a:
             begin(
                 remote(
                     part[a, b], got[a, b], send_p.at[a, b], recv_p.at[a, b], groups[a] * M + m, t
@@ -263,9 +312,12 @@
             (a, b)
             for a in range(G)
             for b in range(G)
-            if max(plan.stage(a), plan.stage(b)) == stage
+            if plan.wave(a, b) == stage
         ]
-        for a, b in sorted(todo, key=lambda ab: (wanted.index(ab[0] ^ ab[1]), -ab[0])):
+        for a, b in [p for p in todo if plan.term_first(*p)]:
+            pair(a, b)
+        rest = [p for p in todo if not plan.term_first(*p)]
+        for a, b in sorted(rest, key=lambda ab: (wanted.index(ab[0] ^ ab[1]), -ab[0])):
             pair(a, b)
 
     to_scalars.wait()
@@ -291,32 +343,50 @@
     if second:
         pairs(2)
 
-    def over_term(source, landing, ssem, rsem):
-        for o in range(1, T):
-            p = term_peer(o)
+    def pass_early(wave):
+        for w, a in [key for key in plan.sets() if key[0] == wave]:
+            for o in range(1, T):
+                remote(
+                    early[w, a].at[:, pl.ds(t * SR, SR), :], early_z[w, a].at[o - 1],
+                    send_ez.at[w - 1, a, o], recv_ez.at[w - 1, a, o], d, term_peer(o),
+                ).wait_recv()
+            for i in range(len(plan.blocks(w, a))):
+                total = early[w, a][i, pl.ds(pl.multiple_of(t * SR, SR), SR), :]
+                for o in range(1, T):
+                    total = total + early_z[w, a][o - 1, i]
+                early_sum[w, a][i] = total
             begin(
                 remote(
-                    source.at[:, pl.ds(p * SR, SR), :], landing.at[o - 1], ssem.at[o], rsem.at[o], d, p
+                    early_sum[w, a], early_xy[w, a], send_ex.at[w - 1, a], recv_ex.at[w - 1, a],
+                    groups[a] * M + m, t,
                 )
             )
 
+    pass_early(1)
     for b in wanted:
-        for a in range(1, G):
+        direct = [a for a in range(1, G) if not plan.term_first(a, a ^ b)]
+        for a in direct:
             remote(
                 part[a, a ^ b], got[a, a ^ b], send_p.at[a, a ^ b], recv_p.at[a, a ^ b],
                 groups[a] * M + m, t,
             ).wait_recv()
         for i in range(plan.count(b)):
             total = part[0, b][i]
-            for a in range(1, G):
+            for a in direct:
                 total = total + got[a, a ^ b][i]
             whole[b][i] = total
         over_term(whole[b], got_z[b], send_z.at[b], recv_z.at[b])
+    pass_early(2)
 
     def mirror_member(b, i):
         return 2 * i + lax.rem(m + jnp.where(groups[b] < g, 1, 0), 2)
 
     lane_set = lax.div(lax.broadcasted_iota(jnp.int32, (max(SR // T, 1), R), 1), SR)
+    for w, a in plan.sets():
+        remote(
+            early_sum[w, a], early_xy[w, a], send_ex.at[w - 1, a], recv_ex.at[w - 1, a],
+            groups[a] * M + m, t,
+        ).wait_recv()
     sums = {}
     for b in wanted:
         for o in range(1, T):
@@ -328,6 +398,10 @@
             total = whole[b][i, pl.ds(pl.multiple_of(t * SR, SR), SR), :]
             for o in range(1, T):
                 total = total + got_z[b][o - 1, i]
+            for a in range(1, G):
+                if plan.term_first(a, a ^ b):
+                    wave = plan.wave(a, a ^ b)
+                    total = total + early_xy[wave, a][plan.blocks(wave, a).index((a ^ b, i))]
             sums[b, i] = total
             if plan.mirrored and b:
                 upright = jnp.concatenate([total] * T, axis=0).T
@@ -396,8 +470,13 @@
     many = lambda *shape: pltpu.SemaphoreType.DMA(shape)
     buffer = lambda *shape: pltpu.VMEM(tuple(max(n, 1) for n in shape), jnp.float32)
     scratch = [pltpu.VMEM((M * (N + 1), R, L), doc_tiles.dtype) for _ in range(G)]
-    scratch += [buffer(plan.count(a ^ b), R, R) for a in range(G) for b in range(G)]
-    scratch += [buffer(plan.count(a ^ b), R, R) for a in range(1, G) for b in range(G)]
+    numbers = [len(plan.blocks(*key)) for key in plan.sets()]
+    scratch += [buffer(plan.count(a ^ b), R, R) for a, b in plan.direct()]
+    scratch += [buffer(plan.count(a ^ b), R, R) for a, b in plan.direct() if a]
+    scratch += [buffer(n, R, R) for n in numbers]
+    scratch += [buffer(T - 1, n, SR, R) for n in numbers]
+    scratch += [buffer(n, SR, R) for n in numbers]
+    scratch += [buffer(n, SR, R) for n in numbers]
     scratch += [buffer(plan.count(b), R, R) for b in range(G)]
     scratch += [buffer(T - 1, plan.count(b), SR, R) for b in range(G)]
     if plan.mirrored:
@@ -413,7 +492,7 @@
         many(G, plan.parts), many(G, M, plan.parts), many(G, M, plan.parts),
         many(T), many(T), many(D), many(D),
         many(G, G), many(G, G), many(G, M, T), many(G, M, T),
-        many(G, T), many(G, T),
+        many(G, T), many(G, T), many(2, G, T), many(2, G, T), many(2, G), many(2, G),
     ]
     return pl.pallas_call(
         functools.partial(body, plan),

time: 74.1 us -> 71.8 us (0.969)
  Pallas kernels: 72.4 us -> 70 us
    pallas_call x1, Pallas kernels: 72.4 us -> 70 us  [shards(): pl.pallas_call(functools.partial(body, plan), out_shape=jax.ShapeDtypeStr...]
where the time goes in v1:
time: 71.8 us; the launch traced here: 71.6 us
  Pallas kernels  70 us (97%)
  local copies, waits for them, and re-layouts  1.57 us (2%)
    pallas_call x1, Pallas kernels, shards(): pl.pallas_call(functools.partial(body, plan), out_shape=jax.ShapeDtypeStr...  70 us
    unnamed x1, local copies, waits for them, and re-layouts  1.57 us

profile of v1, /device:TPU:0, one launch (start us, length us, event | category | flops | bytes accessed | tf_op | source)
XLA Modules:
  0.0 71.6 jit_solution(12254264002904039899)
XLA Ops:
  0.0 70.0 %shard_map.28 = f32[32,1024]{1,0:T(8,128)} custom-call(s32[8,24]{1,0:T(8,128)} %names.1, bf16[3072,512]{1,0:T(8,128)(2,1)} %bitcast.1), custom_call_target="tpu_custom_call" | custom-call | flops 3221225472 | bytes 3276800 | tf_op jit(solution)/shard_map/pallas_call | solution.py:497
  70.1 1.6 %copy.4 = f32[32,1024]{1,0:T(8,128)} copy(f32[32,1024]{1,0:T(8,128)} %shard_map.28) | data formatting | bytes 262144

commit v2 on v1

--- a/solution.py
+++ b/solution.py
@@ -48,6 +48,8 @@
         return a > 0 and (self.wave(a, b) == 1 or a == b)
 
     def blocks(self, wave, a):
+        if wave == 0:
+            return []
         return [
             (b, i)
             for b in range(self.G)
@@ -224,14 +226,15 @@
             send_range(o, h)
 
     for o in range(G):
-        tiles[o][m * (N + 1) + N] = jnp.zeros((R, L), docs.dtype)
+        for member in range(M):
+            tiles[o][member * (N + 1) + N] = jnp.zeros((R, L), docs.dtype)
     same = lax.broadcasted_iota(jnp.int32, (N, N), 0) == lax.broadcasted_iota(jnp.int32, (N, N), 1)
     place = lax.broadcasted_iota(jnp.int32, (N, N), 0)
-    for a in range(G):
-        line = names[pl.ds(groups[a] * M + m, 1), :]
-        upright = jnp.sum(jnp.where(same, line, 0), axis=1, keepdims=True)
-        for c in range(D):
-            found = jnp.where(upright == names[c : c + 1, :], place, N)
+    for c in range(D):
+        upright = jnp.sum(jnp.where(same, names[c : c + 1, :], 0), axis=1, keepdims=True)
+        for a in range(G):
+            line = names[pl.ds(groups[a] * M + m, 1), :]
+            found = jnp.where(upright == line, place, N)
             table_rows[a * D + c : a * D + c + 1, 0:N] = jnp.min(found, axis=0, keepdims=True)
     to_scalars = pltpu.make_async_copy(table_rows, table, table_sem)
     to_scalars.start()
@@ -269,56 +272,64 @@
                 )
             )
 
-    def pair(a, b):
-        wave = plan.wave(a, b)
-        if plan.term_first(a, b):
-            target, base = early[wave, a], plan.blocks(wave, a).index((b, 0))
-        else:
-            target, base = part[a, b], 0
-
-        def one(i, carry):
+    def products(a, wanted_blocks):
+        own = jnp.concatenate([tiles[a][m * (N + 1) + e] for e in range(N)], axis=1)
+        others = []
+        for b, i, target, place in wanted_blocks:
             member = i if a == b else column_member(groups[a], groups[b], i)
             line = a * D + groups[b] * M + member
-            left = jnp.concatenate(
-                [tiles[a][m * (N + 1) + table[line, e]] for e in range(N)], axis=1
-            )
-            right = jnp.concatenate([tiles[b][member * (N + 1) + e] for e in range(N)], axis=1)
-            target[base + i] = lax.dot_general(
-                left, right, (((1,), (1,)), ((), ())), preferred_element_type=jnp.float32
-            )
-            return carry
-
-        number = plan.count(a ^ b)
-        if number == 1:
-            one(0, 0)
+            others.append(
+                jnp.concatenate(
+                    [tiles[b][member * (N + 1) + table[line, e]] for e in range(N)], axis=1
+                )
+            )
+        result = lax.dot_general(
+            jnp.concatenate(others, axis=0), own, (((1,), (1,)), ((), ())),
+            preferred_element_type=jnp.float32,
+        )
+        for k, (b, i, target, place) in enumerate(wanted_blocks):
+            target[place] = result[k * R : (k + 1) * R].T
+
+    def rows_of(wave, a):
+        columns = [b for b in range(G) if plan.wave(a, b) == wave]
+        if not columns:
+            return
+        jobs = []
+        for b in columns:
+            if plan.term_first(a, b):
+                target, base = early[wave, a], plan.blocks(wave, a).index((b, 0))
+            else:
+                target, base = part[a, b], 0
+            jobs.append((b, target, base))
+        if sum(plan.count(a ^ b) for b in columns) <= 8:
+            products(
+                a, [(b, i, x, base + i) for b, x, base in jobs for i in range(plan.count(a ^ b))]
+            )
         else:
-            lax.fori_loop(0, number, one, 0)
-        if plan.term_first(a, b):
-            if plan.blocks(wave, a)[-1][0] == b:
-                over_term(
-                    early[wave, a], early_z[wave, a], send_ez.at[wave - 1, a], recv_ez.at[wave - 1, a]
+            for b, x, base in jobs:
+                def one(i, carry, b=b, x=x, base=base):
+                    products(a, [(b, i, x, base + i)])
+                    return carry
+
+                lax.fori_loop(0, plan.count(a ^ b), one, 0)
+        if plan.blocks(wave, a):
+            over_term(
+                early[wave, a], early_z[wave, a], send_ez.at[wave - 1, a], recv_ez.at[wave - 1, a]
+            )
+        for b in columns:
+            if a and not plan.term_first(a, b):
+                begin(
+                    remote(
+                        part[a, b], got[a, b], send_p.at[a, b], recv_p.at[a, b],
+                        groups[a] * M + m, t,
+                    )
                 )
-        elif a:
-            begin(
-                remote(
-                    part[a, b], got[a, b], send_p.at[a, b], recv_p.at[a, b], groups[a] * M + m, t
-                )
-            )
 
     wanted = list(range(1, G)) + [0]
 
-    def pairs(stage):
-        todo = [
-            (a, b)
-            for a in range(G)
-            for b in range(G)
-            if plan.wave(a, b) == stage
-        ]
-        for a, b in [p for p in todo if plan.term_first(*p)]:
-            pair(a, b)
-        rest = [p for p in todo if not plan.term_first(*p)]
-        for a, b in sorted(rest, key=lambda ab: (wanted.index(ab[0] ^ ab[1]), -ab[0])):
-            pair(a, b)
+    def pairs(wave):
+        for a in sorted(range(G), key=lambda a: (a == 0, -plan.stage(a))):
+            rows_of(wave, a)
 
     to_scalars.wait()
     take_over(0)

time: 71.8 us -> 74 us (1.031)
  Pallas kernels: 70 us -> 72.2 us
    pallas_call x1, Pallas kernels: 70 us -> 72.2 us  [shards(): pl.pallas_call(functools.partial(body, plan), out_shape=jax.ShapeDtypeStr...]
where the time goes in v2:
time: 74 us; the launch traced here: 73.8 us
  Pallas kernels  72.2 us (98%)
  local copies, waits for them, and re-layouts  1.57 us (2%)
    pallas_call x1, Pallas kernels, shards(): pl.pallas_call(functools.partial(body, plan), out_shape=jax.ShapeDtypeStr...  72.2 us
    unnamed x1, local copies, waits for them, and re-layouts  1.57 us

profile of v2, /device:TPU:0, one launch (start us, length us, event | category | flops | bytes accessed | tf_op | source)
XLA Modules:
  0.0 73.8 jit_solution(11809575435496015240)
XLA Ops:
  0.0 72.2 %shard_map.28 = f32[32,1024]{1,0:T(8,128)} custom-call(s32[8,24]{1,0:T(8,128)} %names.1, bf16[3072,512]{1,0:T(8,128)(2,1)} %bitcast.1), custom_call_target="tpu_custom_call" | custom-call | flops 3221225472 | bytes 3276800 | tf_op jit(solution)/shard_map/pallas_call | solution.py:508
  72.2 1.6 %copy.4 = f32[32,1024]{1,0:T(8,128)} copy(f32[32,1024]{1,0:T(8,128)} %shard_map.28) | data formatting | bytes 262144

commit v3 on v1

--- a/solution.py
+++ b/solution.py
@@ -34,8 +34,8 @@
             G > 1 and self.M % 2 == 0 and R == LANES and self.SR % T == 0 and self.SR // T % 8 == 0
         )
         self.H = self.M // 2 if self.mirrored else self.M
-        self.parts = 2 if N % 2 == 0 else 1
-        self.step = N // self.parts
+        self.parts = 2 if R % 32 == 0 else 1
+        self.step = R // self.parts
         self.rows = 16 if R % 16 == 0 else R
 
     def count(self, o):
@@ -121,7 +121,7 @@
     parts, step = plan.parts, plan.step
 
     def slot(o, member, h):
-        return tiles[o].at[pl.ds(member * (N + 1) + h * step, step)]
+        return tiles[o].at[pl.ds(member * (N + 1), N), pl.ds(h * step, step), :]
 
     def cut(group):
         if G == 1:
@@ -153,7 +153,7 @@
     def send_range(o, h):
         return begin(
             remote(
-                ranges[o].at[pl.ds(h * step, step)], slot(o, m, h), send_a.at[o, h],
+                ranges[o].at[:, pl.ds(h * step, step), :], slot(o, m, h), send_a.at[o, h],
                 recv_a.at[o, m, h], groups[o] * M + m, t,
             )
         )
@@ -182,8 +182,10 @@
         ).wait_recv()
         hand_on(o, h)
 
-    def slots_first(o):
-        loads[o].wait()
+    def slots_first(o, h):
+        if h == 0:
+            loads[o].wait()
+        few = step // plan.rows
 
         def some_rows(k, carry):
             rows = pl.ds(pl.multiple_of(k * plan.rows, plan.rows), plan.rows)
@@ -196,7 +198,7 @@
                 tiles[0][pl.ds(m * (N + 1), N), rows, :] = value
             return carry
 
-        lax.fori_loop(0, R // plan.rows, some_rows, 0)
+        lax.fori_loop(h * few, (h + 1) * few, some_rows, 0)
 
     size = plan.rows * N
     origin = jnp.concatenate(
@@ -207,21 +209,22 @@
 
     first_sends = []
     if first:
-        slots_first(first[0])
+        slots_first(first[0], 0)
     if greeted:
         pl.semaphore_wait(barrier, len(greeted))
-    for o in first:
-        if o != first[0]:
-            slots_first(o)
-        for h in range(parts):
+    for h in range(parts):
+        for o in first:
+            if (o, h) != (first[0], 0):
+                slots_first(o, h)
             first_sends.append(send_range(o, h))
-    slots_first(0)
     for h in range(parts):
+        slots_first(0, h)
         hand_on(0, h)
     for o in second:
-        slots_first(o)
-        for h in range(parts - 1):
-            send_range(o, h)
+        for h in range(parts):
+            slots_first(o, h)
+            if h < parts - 1:
+                send_range(o, h)
 
     for o in range(G):
         tiles[o][m * (N + 1) + N] = jnp.zeros((R, L), docs.dtype)

time: 71.8 us -> 77.4 us (1.078)
  Pallas kernels: 70 us -> 75.7 us
    pallas_call x1, Pallas kernels: 70 us -> 75.7 us  [shards(): pl.pallas_call(functools.partial(body, plan), out_shape=jax.ShapeDtypeStr...]
where the time goes in v3:
time: 77.4 us; the launch traced here: 77.2 us
  Pallas kernels  75.7 us (98%)
  local copies, waits for them, and re-layouts  1.57 us (2%)
    pallas_call x1, Pallas kernels, shards(): pl.pallas_call(functools.partial(body, plan), out_shape=jax.ShapeDtypeStr...  75.7 us
    unnamed x1, local copies, waits for them, and re-layouts  1.57 us

profile of v3, /device:TPU:0, one launch (start us, length us, event | category | flops | bytes accessed | tf_op | source)
XLA Modules:
  0.0 77.2 jit_solution(12907622639821987371)
XLA Ops:
  0.0 75.7 %shard_map.28 = f32[32,1024]{1,0:T(8,128)} custom-call(s32[8,24]{1,0:T(8,128)} %names.1, bf16[3072,512]{1,0:T(8,128)(2,1)} %bitcast.1), custom_call_target="tpu_custom_call" | custom-call | flops 3221225472 | bytes 3276800 | tf_op jit(solution)/shard_map/pallas_call | solution.py:500
  75.7 1.6 %copy.4 = f32[32,1024]{1,0:T(8,128)} copy(f32[32,1024]{1,0:T(8,128)} %shard_map.28) | data formatting | bytes 262144

commit v4 on v1

--- a/solution.py
+++ b/solution.py
@@ -34,7 +34,7 @@
             G > 1 and self.M % 2 == 0 and R == LANES and self.SR % T == 0 and self.SR // T % 8 == 0
         )
         self.H = self.M // 2 if self.mirrored else self.M
-        self.parts = 2 if N % 2 == 0 else 1
+        self.parts = 1
         self.step = N // self.parts
         self.rows = 16 if R % 16 == 0 else R
 

time: 71.8 us -> 72 us (level)
  no operation moved by 1% of the time
where the time goes in v4:
time: 72 us; the launch traced here: 71.9 us
  Pallas kernels  70.3 us (98%)
  local copies, waits for them, and re-layouts  1.57 us (2%)
    pallas_call x1, Pallas kernels, shards(): pl.pallas_call(functools.partial(body, plan), out_shape=jax.ShapeDtypeStr...  70.3 us
    unnamed x1, local copies, waits for them, and re-layouts  1.57 us

profile of v4, /device:TPU:0, one launch (start us, length us, event | category | flops | bytes accessed | tf_op | source)
XLA Modules:
  0.0 71.9 jit_solution(14840324723341769199)
XLA Ops:
  0.0 70.3 %shard_map.28 = f32[32,1024]{1,0:T(8,128)} custom-call(s32[8,24]{1,0:T(8,128)} %names.1, bf16[3072,512]{1,0:T(8,128)(2,1)} %bitcast.1), custom_call_target="tpu_custom_call" | custom-call | flops 3221225472 | bytes 3276800 | tf_op jit(solution)/shard_map/pallas_call | solution.py:497
  70.3 1.6 %copy.4 = f32[32,1024]{1,0:T(8,128)} copy(f32[32,1024]{1,0:T(8,128)} %shard_map.28) | data formatting | bytes 262144
